TPU v7x, 32 devices: a whole 2x2x4 slice. The times are simulated.
32 devices in a mesh: date: 8 (over y, x, core), az: 4 (over z).
Axes of the slice: x: 2, y: 2, z: 4, core: 2. Of those that a mesh axis runs over, the one named last changes fastest.
Arguments:
- slc: bfloat16 [16, 2, 256, 3072], P('date', None, 'az'), may hold values from -12 to 12
- az_shift: int32 [16], P('date'), may hold values from -4 to 4, as said below
- rg_shift: int32 [16], P('date'), may hold values from -4 to 4, as said below
- az_frac: int32 [16], P('date'), may hold values from 0 to 15
- rg_frac: int32 [16], P('date'), may hold values from 0 to 15
Outputs:
- coherence: bfloat16 [192, 64, 2, 16], P('date', 'az')
- mean_coherence: float32 [192, 64], P('date', 'az')
Inputs may be any that keep to these rules, and one draw needn't show every extreme that they name: `az_shift`: date 0 has offset 0; some date has offset 4 and some -4. `rg_shift`: date 0 has offset 0; some date has offset 4 and some -4.
All inputs are finite; a program needn't handle non-finite values.
Results may differ from a plain program's by a relative error of at most 0.0035.
Values may be sent and summed in bfloat16 or wider, within the bound.
A program may use at most 64 MiB of HBM per device.

v0:
```python
import jax
import jax.numpy as jnp
from jax import lax
from jax.sharding import PartitionSpec as P

TAPS = 8
KBANK = 16
MAXOFF = 4
LOOK_AZ = 4
LOOK_RG = 16
WINDOW = 7


EPS = 1e-06


def extended(cells, sides, width):
    for axis, dim in sides:
        count = lax.axis_size(axis)
        ends = count - 1
        head = lax.slice_in_dim(cells, 0, width, axis=dim)
        tail = lax.slice_in_dim(cells, cells.shape[dim] - width, cells.shape[dim], axis=dim)
        cells = jnp.concatenate(
            [
                lax.ppermute(tail, axis, [(i, (i + 1) % count) for i in range(ends)]),
                cells,
                lax.ppermute(head, axis, [((i + 1) % count, i) for i in range(ends)]),
            ],
            axis=dim,
        )
    return cells


def spread(value, axis, source):
    kept = jnp.where(lax.axis_index(axis) == source, value, 0).astype(value.dtype)
    return lax.psum(kept, axis)


def for_sending(x):
    return jax.tree.map(lambda a: a.astype(jnp.bfloat16) if a.dtype == jnp.float32 else a, x)


def kernel_bank():
    fraction = jnp.arange(KBANK, dtype=jnp.float32)[:, None] / KBANK
    tap_place = jnp.arange(TAPS, dtype=jnp.float32)[None, :]
    offset = tap_place - (TAPS // 2 - 1) - fraction
    shaped = jnp.sinc(offset) * (0.5 + 0.5 * jnp.cos(jnp.pi * offset / (TAPS // 2 + 0.5)))
    return shaped / jnp.sum(shaped, axis=1, keepdims=True)


def pick_weights(indices, bank):
    selector = (indices[:, None] == jnp.arange(KBANK, dtype=jnp.int32)[None, :]).astype(jnp.float32)
    return jnp.dot(selector, bank, precision=lax.Precision.HIGHEST)


def looks_of(values):
    lead = values.shape[:-2]
    rows_in, cols_in = (values.shape[-2], values.shape[-1])
    boxed = values.reshape(lead + (rows_in // LOOK_AZ, LOOK_AZ, cols_in // LOOK_RG, LOOK_RG))
    return jnp.mean(boxed, axis=(-3, -1))


def window_sum(padded):
    radius = WINDOW // 2
    rows_out = padded.shape[-2] - 2 * radius
    cols_out = padded.shape[-1] - 2 * radius
    across = padded[..., 0:rows_out, :]
    for offset_row in range(1, WINDOW):
        across = across + padded[..., offset_row : offset_row + rows_out, :]
    total = across[..., 0:cols_out]
    for offset_col in range(1, WINDOW):
        total = total + across[..., offset_col : offset_col + cols_out]
    return total


def form_looks(
    padded, center, rim_width, extra_rows, rows_out, az_shift, rg_shift, az_weights, rg_weights
):
    margin = MAXOFF + TAPS // 2
    n_dates, rows_in, n_cols = (padded.shape[0], padded.shape[2], padded.shape[3])
    widened = jnp.pad(padded, ((0, 0), (0, 0), (0, 0), (margin, margin)))
    center_re = center[0].astype(jnp.float32)
    center_im = center[1].astype(jnp.float32)
    pieces = []
    for date_pos in range(n_dates):
        ranged = jnp.zeros((2, rows_in, n_cols), jnp.float32)
        for tap_place in range(TAPS):
            start = margin + rg_shift[date_pos] + tap_place - (TAPS // 2 - 1)
            ranged = ranged + rg_weights[date_pos, tap_place] * lax.dynamic_slice_in_dim(
                widened[date_pos], start, n_cols, 2
            ).astype(jnp.float32)
        resampled = jnp.zeros((2, rows_out, n_cols), jnp.float32)
        for tap_place in range(TAPS):
            start = rim_width - extra_rows + az_shift[date_pos] + tap_place - (TAPS // 2 - 1)
            resampled = resampled + az_weights[date_pos, tap_place] * lax.dynamic_slice_in_dim(
                ranged, start, rows_out, 1
            )
        real_part = center_re * resampled[0] + center_im * resampled[1]
        imag_part = center_im * resampled[0] - center_re * resampled[1]
        power_sec = resampled[0] * resampled[0] + resampled[1] * resampled[1]
        pieces.append(looks_of(jnp.stack([real_part, imag_part, power_sec])))
    power_ref = looks_of(center_re * center_re + center_im * center_im)[None]
    return jnp.concatenate(pieces + [power_ref], axis=0)


def per_pixel(piece):
    as_float = piece.astype(jnp.float32)
    magnitude = jnp.sqrt(
        as_float[:, :, 0] * as_float[:, :, 0] + as_float[:, :, 1] * as_float[:, :, 1]
    )
    return (piece, jnp.mean(magnitude, axis=-1))


def body(slc, az_shift, rg_shift, az_frac, rg_frac):
    n_dates, n_rows, n_cols = (slc.shape[0], slc.shape[2], slc.shape[3])
    bank = kernel_bank()
    az_weights = pick_weights(az_frac, bank)
    rg_weights = pick_weights(rg_frac, bank)
    radius = WINDOW // 2
    margin = MAXOFF + TAPS // 2
    look_rows = n_rows // LOOK_AZ
    padded = extended(slc, (("az", 2),), margin)
    center = spread(slc[0], "date", 0)
    stacked = form_looks(
        padded, center, margin, 0, n_rows, az_shift, rg_shift, az_weights, rg_weights
    )
    stacked = extended(for_sending(stacked), (("az", 1),), radius).astype(stacked.dtype)
    widened = jnp.pad(stacked, ((0, 0), (0, 0), (radius, radius)))
    summed = window_sum(widened)
    look_cols = summed.shape[2]
    per_date = summed[:-1].reshape(n_dates, 3, look_rows, look_cols)
    scale = 1.0 / jnp.sqrt(summed[-1][None] * per_date[:, 2] + EPS)
    gamma = jnp.stack([per_date[:, 0] * scale, per_date[:, 1] * scale], axis=1).astype(jnp.bfloat16)
    outgoing = jnp.transpose(gamma, (3, 2, 1, 0))
    coherence, mean_coherence = per_pixel(
        lax.all_to_all(outgoing, "date", split_axis=0, concat_axis=3, tiled=True)
    )
    return (coherence, mean_coherence)


def solution(mesh):
    placed = (P("date", None, "az", None), P("date"), P("date"), P("date"), P("date"))
    return jax.shard_map(
        body,
        mesh=mesh,
        in_specs=placed,
        out_specs=(P("date", "az", None, None), P("date", "az")),
        check_vma=False,
    )
```

profile of v0, /device:TPU:0, one launch (start us, length us, event | category | flops | bytes accessed | tf_op | source)
XLA Modules:
  0.0 194.3 jit_solution(12457617068868251245)
XLA Ops:
  9.7 5.6 %collective-permute-start = (bf16[2,2,8,3072]{3,2,1,0:T(8,128)(2,1)S(1)}, bf16[2,2,8,3072]{3,2,1,0:T(8,128)(2,1)S(1)}, u32[]{:S(2)}, u32[]{:S(2)}) collective-permute-start(bf16[2,2,8,3072]{3,2,1,0:T(8,128)(2,1)S(1)} %get-tuple-element.16), channel_id=1, source_target_pairs={{0,1},{1,2},{2,3},{4,5},{5,6},{6,7},{8,9},{9,10},{10,11},{12,13},{... | collective-permute-start | bytes 589832 | tf_op jit(solution)/shard_map/ppermute | solution.py:25
  15.3 2.1 %select_bitcast_fusion = bf16[2,64,3072]{2,1,0:T(8,128)(2,1)} fusion(bf16[2,2,64,3072]{3,2,1,0:T(8,128)(2,1)} %param.5, pred[]{:T(512)S(6)} %eq.51), kind=kLoop, calls=%fused_computation.31 | loop fusion | flops 393216 | bytes 1572865 | tf_op jit(solution)/shard_map/jit(_where)/select_n | solution.py:35
  61.6 10.1 %add_add_fusion.1 = f32[1,2,80,3072]{3,2,1,0:T(8,128)S(1)} fusion(bf16[1,2,80,3088]{3,2,1,0:T(8,128)(2,1)S(1)} %get-tuple-element.12, s32[]{:T(128)S(6)} %select_n.154, f32[]{:T(128)} %bitcast.23, s32[]{:T(128)S(6)} %select_n.153, f32[]{:T(128)} %bitcast.20, s32[]{:T(128)S(6)} %select_n.152, f32[]{:T(128)} %bitcast.17, s32[]{:T(128)S(6)} %select_n.151, ...), kind=kLoop, calls=%fused_computation.11 | loop fusion | flops 11304960 | bytes 9830464 | tf_op jit(solution)/shard_map/add | solution.py:89
  71.7 10.1 %add_add_fusion = f32[1,2,80,3072]{3,2,1,0:T(8,128)S(1)} fusion(bf16[1,2,80,3088]{3,2,1,0:T(8,128)(2,1)S(1)} %get-tuple-element.13, s32[]{:T(128)S(6)} %select_n.170, f32[]{:T(128)} %bitcast.73, s32[]{:T(128)S(6)} %select_n.169, f32[]{:T(128)} %bitcast.70, s32[]{:T(128)S(6)} %select_n.168, f32[]{:T(128)} %bitcast.67, s32[]{:T(128)S(6)} %select_n.167, ...), kind=kLoop, calls=%fused_computation.10 | loop fusion | flops 11304960 | bytes 9830464 | tf_op jit(solution)/shard_map/add | solution.py:89
  81.8 6.7 %bitcast_add_fusion.1 = f32[2,64,3072]{2,1,0:T(8,128)S(1)} fusion(f32[1,2,80,3072]{3,2,1,0:T(8,128)S(1)} %add_add_fusion.1, s32[]{:T(128)S(6)} %select_n.162, s32[]{:T(128)S(6)} %select_n.161, s32[]{:T(128)S(6)} %select_n.160, s32[]{:T(128)S(6)} %select_n.159, s32[]{:T(128)S(6)} %select_n.158, s32[]{:T(128)S(6)} %select_n.157, s32[]{:T(128)S(6)} %select_n.156, ...), kind=kLoop, calls=%fused_computation.13 | loop fusion | flops 5898240 | bytes 14155840 | tf_op jit(solution)/shard_map/add | solution.py:95
  88.5 6.9 %bitcast_add_fusion = f32[2,64,3072]{2,1,0:T(8,128)S(1)} fusion(f32[1,2,80,3072]{3,2,1,0:T(8,128)S(1)} %add_add_fusion, s32[]{:T(128)S(6)} %select_n.178, s32[]{:T(128)S(6)} %select_n.177, s32[]{:T(128)S(6)} %select_n.176, s32[]{:T(128)S(6)} %select_n.175, s32[]{:T(128)S(6)} %select_n.174, s32[]{:T(128)S(6)} %select_n.173, s32[]{:T(128)S(6)} %select_n.172, ...), kind=kLoop, calls=%fused_computation.12 | loop fusion | flops 5898240 | bytes 14155840 | tf_op jit(solution)/shard_map/add | solution.py:95
  95.4 3.1 %fusion.6 = (f32[1,64,3072]{2,1,0:T(8,128)}, f32[1,64,3072]{2,1,0:T(8,128)}, f32[1,64,3072]{2,1,0:T(8,128)}, f32[1,64,3072]{2,1,0:T(8,128)}) fusion(f32[2,64,3072]{2,1,0:T(8,128)S(1)} %bitcast_add_fusion.1, bf16[2,64,3072]{2,1,0:T(8,128)(2,1)} %all-reduce.4.cloned.1.call-done), kind=kLoop, calls=%fused_computation.24 | loop fusion | flops 2752512 | bytes 5505024 | tf_op jit(solution)/shard_map/add | solution.py:98
  98.5 4.9 %add.863 = f32[16,4,192,16]{3,2,1,0:T(8,128)} reshape(f32[1,64,3072]{2,1,0:T(8,128)} %get-tuple-element.18) | data formatting | bytes 1572864 | tf_op jit(solution)/shard_map/add | solution.py:102
  103.4 3.5 %reduce_sum.48 = f32[16,192]{1,0:T(8,128)S(1)} reduce(f32[16,4,192,16]{3,2,1,0:T(8,128)} %add.863, f32[]{:T(128)} %constant.274.clone.1), dimensions={1,3}, to_apply=%region_4.5 | reduce | flops 193536 | bytes 798724 | tf_op jit(solution)/shard_map/reduce_sum | solution.py:60
  107.0 1.5 fusion.8
  108.5 3.8 %stack.36 = f32[1,16,4,192,16]{4,3,2,1,0:T(8,128)} reshape(f32[1,64,3072]{2,1,0:T(8,128)S(1)} %get-tuple-element.15) | data formatting | bytes 1572864 | tf_op jit(solution)/shard_map/stack | solution.py:101
  112.3 5.0 %copy.25 = f32[1,16,4,192,16]{3,4,2,1,0:T(8,128)S(1)} copy(f32[1,16,4,192,16]{4,3,2,1,0:T(8,128)} %stack.36) | data formatting | bytes 1572864 | tf_op jit(solution)/shard_map/stack | solution.py:101
  117.3 3.8 %stack.35 = f32[1,16,4,192,16]{4,3,2,1,0:T(8,128)} reshape(f32[1,64,3072]{2,1,0:T(8,128)S(1)} %copy-done.5) | data formatting | bytes 1572864 | tf_op jit(solution)/shard_map/stack | solution.py:101
  121.1 5.0 %copy.24 = f32[1,16,4,192,16]{3,4,2,1,0:T(8,128)S(1)} copy(f32[1,16,4,192,16]{4,3,2,1,0:T(8,128)} %stack.35) | data formatting | bytes 1572864 | tf_op jit(solution)/shard_map/stack | solution.py:101
  126.1 3.8 %stack.34 = f32[1,16,4,192,16]{4,3,2,1,0:T(8,128)} reshape(f32[1,64,3072]{2,1,0:T(8,128)S(1)} %copy-done.4) | data formatting | bytes 1572864 | tf_op jit(solution)/shard_map/stack | solution.py:101
  130.0 4.9 %copy.23 = f32[1,16,4,192,16]{3,4,2,1,0:T(8,128)S(1)} copy(f32[1,16,4,192,16]{4,3,2,1,0:T(8,128)} %stack.34) | data formatting | bytes 1572864 | tf_op jit(solution)/shard_map/stack | solution.py:101
  134.9 4.9 %stack.32 = f32[1,16,4,192,16]{4,3,2,1,0:T(8,128)} reshape(f32[1,64,3072]{2,1,0:T(8,128)} %get-tuple-element.14) | data formatting | bytes 1572864 | tf_op jit(solution)/shard_map/stack | solution.py:101
  139.8 5.6 %copy.22 = f32[1,16,4,192,16]{3,4,2,1,0:T(8,128)} copy(f32[1,16,4,192,16]{4,3,2,1,0:T(8,128)} %stack.32) | data formatting | bytes 1572864 | tf_op jit(solution)/shard_map/stack | solution.py:101
  145.4 4.9 %stack.31 = f32[1,16,4,192,16]{4,3,2,1,0:T(8,128)} reshape(f32[1,64,3072]{2,1,0:T(8,128)} %get-tuple-element.9) | data formatting | bytes 1572864 | tf_op jit(solution)/shard_map/stack | solution.py:101
  150.3 5.6 %copy.21 = f32[1,16,4,192,16]{3,4,2,1,0:T(8,128)} copy(f32[1,16,4,192,16]{4,3,2,1,0:T(8,128)} %stack.31) | data formatting | bytes 1572864 | tf_op jit(solution)/shard_map/stack | solution.py:101
  156.0 4.9 %stack.30 = f32[1,16,4,192,16]{4,3,2,1,0:T(8,128)} reshape(f32[1,64,3072]{2,1,0:T(8,128)} %get-tuple-element.8) | data formatting | bytes 1572864 | tf_op jit(solution)/shard_map/stack | solution.py:101
  160.9 5.6 %copy.20 = f32[1,16,4,192,16]{3,4,2,1,0:T(8,128)} copy(f32[1,16,4,192,16]{4,3,2,1,0:T(8,128)} %stack.30) | data formatting | bytes 1572864 | tf_op jit(solution)/shard_map/stack | solution.py:101
  170.2 4.5 %collective-permute-start.2 = (bf16[7,3,192]{2,1,0:T(4,128)(2,1)S(1)}, bf16[7,3,192]{2,1,0:T(4,128)(2,1)S(1)}, u32[]{:S(2)}, u32[]{:S(2)}) collective-permute-start(bf16[7,3,192]{2,1,0:T(4,128)(2,1)S(1)} %get-tuple-element.21), channel_id=1, source_target_pairs={{0,1},{1,2},{2,3},{4,5},{5,6},{6,7},{8,9},{9,10},{10,11},{12,13},{... | collective-permute-start | bytes 24200 | tf_op jit(solution)/shard_map/ppermute | solution.py:25
  177.0 8.7 %all_to_all.18 = bf16[8,2,768]{2,1,0:T(2,128)(2,1)S(1)} all-to-all(bf16[8,2,768]{2,1,0:T(2,128)(2,1)S(1)} %reshape.320), channel_id=1, replica_groups=mesh['date'=8,'az'=4] {'date'}, dimensions={0} | all-to-all | bytes 49152 | tf_op jit(solution)/shard_map/all_to_all | solution.py:136
  (63 shorter events, 14.4 us)
Async XLA Ops:
  7.2 53.4 %copy-start = (bf16[2,2,64,3072]{3,2,1,0:T(8,128)(2,1)S(1)}, bf16[2,2,64,3072]{3,2,1,0:T(8,128)(2,1)}, u32[]{:S(2)}) copy-start(bf16[2,2,64,3072]{3,2,1,0:T(8,128)(2,1)} %param.5) | copy-start | bytes 4718596
  7.2 10.3 %copy-start.7 = (s32[2]{0:T(128)S(1)}, s32[2]{0:T(128)}, u32[]{:S(2)}) copy-start(s32[2]{0:T(128)} %param.7) | copy-start | bytes 28
  7.2 12.1 %copy-start.8 = (s32[2]{0:T(128)S(1)}, s32[2]{0:T(128)}, u32[]{:S(2)}) copy-start(s32[2]{0:T(128)} %param.6) | copy-start | bytes 28
  7.2 51.3 %copy-start.9 = (s32[2]{0:T(128)S(1)}, s32[2]{0:T(128)}, u32[]{:S(2)}) copy-start(s32[2]{0:T(128)} %param.9) | copy-start | bytes 28
  7.2 51.5 %copy-start.10 = (s32[2]{0:T(128)S(1)}, s32[2]{0:T(128)}, u32[]{:S(2)}) copy-start(s32[2]{0:T(128)} %param.8) | copy-start | bytes 28
  7.2 88.2 %all-reduce.4.cloned.1.call-start = ((), (), s32[]{:S(2)}) async-start(), calls=%async_computation.1 | async-start | bytes 1572864 | tf_op jit(solution)/shard_map/psum | solution.py:36
  8.4 52.2 %collective-permute-start.1 = (bf16[2,2,8,3072]{3,2,1,0:T(8,128)(2,1)S(1)}, bf16[2,2,8,3072]{3,2,1,0:T(8,128)(2,1)S(1)}, u32[]{:S(2)}, u32[]{:S(2)}) collective-permute-start(bf16[2,2,8,3072]{3,2,1,0:T(8,128)(2,1)S(1)} %get-tuple-element.17), channel_id=1, source_target_pairs={{1,0},{2,1},{3,2},{5,4},{6,5},{7,6},{9,8},{10,9},{11,10},{13,12},{... | collective-permute-start | bytes 589832 | tf_op jit(solution)/shard_map/ppermute | solution.py:27
  9.7 50.9 %collective-permute-start = (bf16[2,2,8,3072]{3,2,1,0:T(8,128)(2,1)S(1)}, bf16[2,2,8,3072]{3,2,1,0:T(8,128)(2,1)S(1)}, u32[]{:S(2)}, u32[]{:S(2)}) collective-permute-start(bf16[2,2,8,3072]{3,2,1,0:T(8,128)(2,1)S(1)} %get-tuple-element.16), channel_id=1, source_target_pairs={{0,1},{1,2},{2,3},{4,5},{5,6},{6,7},{8,9},{9,10},{10,11},{12,13},{... | collective-permute-start | bytes 589832 | tf_op jit(solution)/shard_map/ppermute | solution.py:25
  103.4 3.5 %copy-start.6 = (bf16[2,64,3072]{2,1,0:T(8,128)(2,1)S(1)}, bf16[2,64,3072]{2,1,0:T(8,128)(2,1)}, u32[]{:S(2)}) copy-start(bf16[2,64,3072]{2,1,0:T(8,128)(2,1)} %all-reduce.4.cloned.1.call-done) | copy-start | bytes 2359300
  112.3 5.0 %copy-start.5 = (f32[1,64,3072]{2,1,0:T(8,128)S(1)}, f32[1,64,3072]{2,1,0:T(8,128)}, u32[]{:S(2)}) copy-start(f32[1,64,3072]{2,1,0:T(8,128)} %get-tuple-element.11) | copy-start | bytes 2359300
  121.1 5.0 %copy-start.4 = (f32[1,64,3072]{2,1,0:T(8,128)S(1)}, f32[1,64,3072]{2,1,0:T(8,128)}, u32[]{:S(2)}) copy-start(f32[1,64,3072]{2,1,0:T(8,128)} %get-tuple-element.10) | copy-start | bytes 2359300
  166.5 1.2 copy-start.1
  166.5 1.5 copy-start.2
  166.5 1.9 copy-start.3
  168.9 5.9 %collective-permute-start.3 = (bf16[7,3,192]{2,1,0:T(4,128)(2,1)S(1)}, bf16[7,3,192]{2,1,0:T(4,128)(2,1)S(1)}, u32[]{:S(2)}, u32[]{:S(2)}) collective-permute-start(bf16[7,3,192]{2,1,0:T(4,128)(2,1)S(1)} %get-tuple-element.22), channel_id=1, source_target_pairs={{1,0},{2,1},{3,2},{5,4},{6,5},{7,6},{9,8},{10,9},{11,10},{13,12},{... | collective-permute-start | bytes 24200 | tf_op jit(solution)/shard_map/ppermute | solution.py:27
  170.2 6.0 %collective-permute-start.2 = (bf16[7,3,192]{2,1,0:T(4,128)(2,1)S(1)}, bf16[7,3,192]{2,1,0:T(4,128)(2,1)S(1)}, u32[]{:S(2)}, u32[]{:S(2)}) collective-permute-start(bf16[7,3,192]{2,1,0:T(4,128)(2,1)S(1)} %get-tuple-element.21), channel_id=1, source_target_pairs={{0,1},{1,2},{2,3},{4,5},{5,6},{6,7},{8,9},{9,10},{10,11},{12,13},{... | collective-permute-start | bytes 24200 | tf_op jit(solution)/shard_map/ppermute | solution.py:25
Sparse Core Ops, SparseCore 0:
  17.5 56.2 all-reduce.3
where the time goes:
time: 196 us; the launch traced here: 194 us
  local copies, waits for them, and re-layouts  69.5 us (35%)
  between operations  54.3 us (28%)
  other arithmetic  47.1 us (24%)
  starting transfers between devices  12.7 us (6%)
  blocking collectives  8.73 us (4%)
    another operation x12, local copies, waits for them, and re-layouts, form_looks(): pieces.append(looks_of(jnp.stack([real_part, imag_part, power_sec])))  57.9 us
    add x2, other arithmetic, form_looks(): ranged + rg_weights[date_pos, tap_place] * lax.dynamic_slice_in_dim(widen...  20.2 us
    add x2, other arithmetic, form_looks(): resampled + az_weights[date_pos, tap_place] * lax.dynamic_slice_in_dim(ra...  13.6 us
    ppermute x2, starting transfers between devices, extended(): lax.ppermute(tail, axis, [(i, (i + 1) % count) for i in range(ends)])  10.1 us
    all_to_all x1, blocking collectives, body(): lax.all_to_all(outgoing, 'date', split_axis=0, concat_axis=3, tiled=True)  8.73 us
    add x1, local copies, waits for them, and re-layouts, form_looks(): power_ref = looks_of(center_re * center_re + center_im * center_im)[None]  4.89 us
    add x2, other arithmetic, form_looks(): real_part = center_re * resampled[0] + center_im * resampled[1]  4.65 us
    reduce_sum x3, other arithmetic, looks_of(): return jnp.mean(boxed, axis=(-3, -1))  4.42 us
  transfers between devices with their start and end apart: 5, of which 1 were waited for; matrix products, arithmetic and copies ran while one was open for 21% of the time, Pallas kernels for 0%

commit v1 on v0

v1 whole, which is shorter than its diff:
```python
import functools

import jax
import jax.numpy as jnp
import numpy as np
from jax import lax
from jax.experimental import pallas as pl
from jax.experimental.pallas import tpu as pltpu
from jax.sharding import PartitionSpec as P

TAPS = 8
KBANK = 16
MAXOFF = 4
LOOK_AZ = 4
LOOK_RG = 16
WINDOW = 7
EPS = 1e-06

LEFT = TAPS // 2 - 1
RADIUS = WINDOW // 2
RIM = MAXOFF + TAPS // 2
LANE = 128
BLOCK = 2 * LANE
CHUNK = 16
MESH = pl.DeviceIdType.MESH


def kernel_bank():
    fraction = np.arange(KBANK, dtype=np.float64)[:, None] / KBANK
    offset = np.arange(TAPS, dtype=np.float64)[None, :] - LEFT - fraction
    shaped = np.sinc(offset) * (0.5 + 0.5 * np.cos(np.pi * offset / (TAPS // 2 + 0.5)))
    return (shaped / shaped.sum(axis=1, keepdims=True)).astype(np.float32)


def column_boxes(cols, lanes):
    look = np.arange(cols)[:, None] // LOOK_RG
    place = np.arange(lanes)[None, :]
    inside = (np.abs(look - place) <= RADIUS) & (place < cols // LOOK_RG)
    return jnp.asarray(inside, jnp.bfloat16)


def row_boxes(kinds, rows):
    looks = rows // LOOK_AZ
    kind_in = np.arange(kinds * rows) // rows
    look_in = (np.arange(kinds * rows) % rows) // LOOK_AZ
    kind_out = np.concatenate([np.repeat(np.arange(kinds), looks)] + [np.repeat(np.arange(kinds), 8)] * 2)
    look_out = np.concatenate(
        [
            np.tile(np.arange(looks), kinds),
            np.tile(np.arange(8) - 8, kinds),
            np.tile(np.arange(8) + looks, kinds),
        ]
    )
    inside = (kind_in[None] == kind_out[:, None]) & (np.abs(look_in[None] - look_out[:, None]) <= RADIUS)
    return jnp.asarray(inside / (LOOK_AZ * LOOK_RG), jnp.bfloat16)


def two_terms(x):
    high = x.astype(jnp.bfloat16)
    return high, (x - high.astype(jnp.float32)).astype(jnp.bfloat16)


def banded(tap, weights):
    out = jnp.zeros(tap.shape, jnp.float32)
    for j in range(TAPS):
        out = jnp.where(tap == j, weights[j], out)
    return out


def dot(a, b):
    return jnp.dot(a, b, preferred_element_type=jnp.float32)


def kernel(
    n, n_az, dates, rows, cols,
    az_shift, rg_shift, az_frac, rg_frac, bank, slc, boxes_hbm, row_box,
    coh_ref, mean_ref,
    own, rim_out, rim_in, center, boxes, toep, azm, ranged, sec, prod, looks, edge_out, edge_in,
    strip_out, strip_in,
    load_sem, box_sem, own_sem, rim_send, rim_recv, c_ring, c_core, c_recv, e_send, e_recv, s_send, s_recv,
):
    me, az = lax.axis_index("date"), lax.axis_index("az")
    pair = 2 if n % 2 == 0 and n >= 4 else 1
    chips = n // pair
    chip, core = me // pair, me % pair

    def snake(p):
        return (p // 2) * 2 + (p + p // 2) % 2

    pos = snake(chip)
    onward = snake((pos + 1) % chips) * pair + core
    back = snake((pos + chips - 1) % chips) * pair + core
    up, down = jnp.maximum(az - 1, 0), jnp.minimum(az + 1, n_az - 1)
    has_up, has_down = az > 0, az < n_az - 1

    kinds = 3 * dates + 1
    look_rows = rows // LOOK_AZ
    strip = cols // LOOK_RG // n
    n_blocks = cols // BLOCK
    inner = pl.ds(LANE, cols)

    loads = [
        pltpu.make_async_copy(slc.at[d, c], own.at[d, pl.ds(c * rows, rows), inner], load_sem.at[d, c])
        for d in range(dates)
        for c in range(2)
    ]
    for load in loads:
        load.start()
    box_load = pltpu.make_async_copy(boxes_hbm, boxes, box_sem)
    box_load.start()

    barrier = pltpu.get_barrier_semaphore()

    def greet(s, _):
        pl.semaphore_signal(barrier, inc=1, device_id=((me + s) % n, az), device_id_type=MESH)
        return 0

    lax.fori_loop(1, n, greet, 0)

    @pl.when(has_up)
    def _():
        pl.semaphore_signal(barrier, inc=1, device_id=(me, up), device_id_type=MESH)

    @pl.when(has_down)
    def _():
        pl.semaphore_signal(barrier, inc=1, device_id=(me, down), device_id_type=MESH)

    for d in range(dates):
        for lo in (0, LANE + cols):
            own[d, :, lo : lo + LANE] = jnp.zeros((2 * rows, LANE), jnp.bfloat16)
            for side in range(2):
                rim_in[side, d, :, lo : lo + LANE] = jnp.zeros((2 * RIM, LANE), jnp.bfloat16)

    @pl.when(jnp.logical_not(has_up))
    def _():
        rim_in[0, :, :, LANE : LANE + cols] = jnp.zeros((dates, 2 * RIM, cols), jnp.bfloat16)
        edge_in[0] = jnp.zeros(edge_in.shape[1:], jnp.float32)

    @pl.when(jnp.logical_not(has_down))
    def _():
        rim_in[1, :, :, LANE : LANE + cols] = jnp.zeros((dates, 2 * RIM, cols), jnp.bfloat16)
        edge_in[1] = jnp.zeros(edge_in.shape[1:], jnp.float32)

    for load in loads:
        load.wait()

    for d in range(dates):
        for side, lo in ((0, 0), (1, rows - 16)):
            cut = slice(0, RIM) if side == 0 else slice(16 - RIM, 16)
            both = [
                own[d, c * rows + lo : c * rows + lo + 16, LANE : LANE + cols].astype(jnp.float32)[cut]
                for c in range(2)
            ]
            rim_out[side, d] = jnp.concatenate(both, axis=0).astype(jnp.bfloat16)

    n_here = has_up.astype(jnp.int32) + has_down.astype(jnp.int32)
    pl.semaphore_wait(barrier, n - 1 + n_here)

    def rim_copy(side):
        return pltpu.make_async_remote_copy(
            src_ref=rim_out.at[side],
            dst_ref=rim_in.at[1 - side, :, :, inner],
            send_sem=rim_send.at[side],
            recv_sem=rim_recv.at[1 - side],
            device_id=(me, up if side == 0 else down),
            device_id_type=MESH,
        )

    per_part = rows // CHUNK

    def place(i, part):
        return i % 2, pl.ds(pl.multiple_of((i // 2) * CHUNK + part * (rows // 2), CHUNK), CHUNK)

    def chunk_copy(i, part, source, to, sems):
        c, r = place(i, part)
        return pltpu.make_async_remote_copy(
            src_ref=source.at[c, r, :],
            dst_ref=center.at[c, r, :],
            send_sem=sems.at[part, i],
            recv_sem=c_recv.at[part, i],
            device_id=(to, az),
            device_id_type=MESH,
        )

    is_source = jnp.logical_and(pos == 0, core == 0)
    relay = jnp.logical_and(pos > 0, core == 0)
    sibling = chip * pair + 1
    own_center = pltpu.make_async_copy(slc.at[0], center, own_sem)

    @pl.when(is_source)
    def _():
        for i in range(per_part):
            for part, to in ((0, onward), (1, back)):
                chunk_copy(i, part, slc.at[0], to, c_ring).start()
        for i in range(per_part):
            for part in range(2):
                if pair == 2:
                    chunk_copy(i, part, slc.at[0], sibling, c_core).start()
        own_center.start()

    @pl.when(has_up)
    def _():
        rim_copy(0).start()

    @pl.when(has_down)
    def _():
        rim_copy(1).start()

    def relay_step(t):
        for part, i, last, to in ((0, t - pos, chips - 1, onward), (1, t - (chips - pos), 1, back)):

            @pl.when(relay & (i >= 0) & (i < per_part))
            def _():
                chunk_copy(i, part, center, to, c_ring).wait_recv()

                @pl.when(pos != last)
                def _():
                    chunk_copy(i, part, center, to, c_ring).start()

                if pair == 2:
                    chunk_copy(i, part, center, sibling, c_core).start()

    steps = [functools.partial(relay_step, t) for t in range(1, chips + per_part - 1)]

    for d in range(dates):
        weights = [bank[rg_frac[d], j] for j in range(TAPS)]
        across = lax.broadcasted_iota(jnp.int32, (LANE, LANE), 0) - lax.broadcasted_iota(jnp.int32, (LANE, LANE), 1)
        for b in range(3):
            terms = two_terms(banded(across + (LANE * (b - 1) + LEFT - rg_shift[d]), weights))
            for k in range(2):
                for right in range(2):
                    toep[d, k, LANE * (b + right) : LANE * (b + right + 1), LANE * right : LANE * (right + 1)] = terms[k]
        for k in range(2):
            zero = jnp.zeros((LANE, LANE), jnp.bfloat16)
            toep[d, k, 0:LANE, LANE:] = zero
            toep[d, k, 3 * LANE :, 0:LANE] = zero

    deep = 2 * rows + 4 * RIM
    for d in range(dates):
        weights = [bank[az_frac[d], j] for j in range(TAPS)]
        out = lax.broadcasted_iota(jnp.int32, (2 * rows, deep), 0)
        src = lax.broadcasted_iota(jnp.int32, (2 * rows, deep), 1)
        rim = src - 2 * rows
        in_own = rim < 0
        rim = jnp.maximum(rim, 0)
        rim_row = lax.rem(rim, RIM)
        src_part = jnp.where(in_own, lax.div(src, rows), lax.rem(lax.div(rim, RIM), 2))
        src_row = jnp.where(in_own, lax.rem(src, rows), jnp.where(rim < 2 * RIM, rim_row - RIM, rim_row + rows))
        tap = src_row - lax.rem(out, rows) + (LEFT - az_shift[d])
        tap = jnp.where(src_part == lax.div(out, rows), tap, -1)
        terms = two_terms(banded(tap, weights))
        for k in range(2):
            azm[d, k * 2 * rows : (k + 1) * 2 * rows, :] = terms[k]

    def range_block(k, _):
        window = pl.ds(pl.multiple_of(k * BLOCK, LANE), 2 * BLOCK)
        here = pl.ds(pl.multiple_of(k * BLOCK, LANE), BLOCK)
        for d in range(dates):
            x = own[d, :, window]
            ranged[d, 0 : 2 * rows, here] = (dot(x, toep[d, 0]) + dot(x, toep[d, 1])).astype(jnp.bfloat16)
        return 0

    done = 0
    for t, step in enumerate(steps):
        step()
        until = min(n_blocks, -(-n_blocks * (t + 1) // min(len(steps), 4)))
        if until > done:
            lax.fori_loop(done, until, range_block, 0)
            done = until

    @pl.when(has_up)
    def _():
        rim_copy(1).wait_recv()

    @pl.when(has_down)
    def _():
        rim_copy(0).wait_recv()

    def az_block(k, _):
        window = pl.ds(pl.multiple_of(k * BLOCK, LANE), 2 * BLOCK)
        here = pl.ds(pl.multiple_of(k * BLOCK, LANE), BLOCK)
        for d in range(dates):
            x = jnp.concatenate([rim_in[0, d, :, window], rim_in[1, d, :, window]], axis=0)
            ranged[d, 2 * rows :, here] = (dot(x, toep[d, 0]) + dot(x, toep[d, 1])).astype(jnp.bfloat16)
            both = dot(azm[d], ranged[d, :, here])
            s = both[0 : 2 * rows] + both[2 * rows :]
            sec[d, :, here] = s.astype(jnp.bfloat16)
            power = s[0:rows] * s[0:rows] + s[rows:] * s[rows:]
            prod[(3 * d + 2) * rows : (3 * d + 3) * rows, here] = power.astype(jnp.bfloat16)
        return 0

    lax.fori_loop(0, n_blocks, az_block, 0)

    @pl.when(is_source)
    def _():
        own_center.wait()

    @pl.when(core != 0)
    def _():
        for i in range(per_part):
            for part in range(2):
                chunk_copy(i, part, center, onward, c_ring).wait_recv()

    def cross_block(k, _):
        here = pl.ds(pl.multiple_of(k * BLOCK, LANE), BLOCK)
        e0, e1 = center[0, :, here].astype(jnp.float32), center[1, :, here].astype(jnp.float32)
        for d in range(dates):
            s0 = sec[d, 0:rows, here].astype(jnp.float32)
            s1 = sec[d, rows:, here].astype(jnp.float32)
            prod[3 * d * rows : (3 * d + 1) * rows, here] = (e0 * s0 + e1 * s1).astype(jnp.bfloat16)
            prod[(3 * d + 1) * rows : (3 * d + 2) * rows, here] = (e1 * s0 - e0 * s1).astype(jnp.bfloat16)
        prod[3 * dates * rows :, here] = (e0 * e0 + e1 * e1).astype(jnp.bfloat16)
        return 0

    lax.fori_loop(0, n_blocks, cross_block, 0)

    box_load.wait()
    high, low = two_terms(dot(prod[...], boxes[...]))
    looks[...] = dot(row_box[...], high) + dot(row_box[...], low)
    n_own = kinds * look_rows
    edge_out[0] = looks[n_own : n_own + 8 * kinds, :]
    edge_out[1] = looks[n_own + 8 * kinds :, :]

    def edge_copy(side):
        return pltpu.make_async_remote_copy(
            src_ref=edge_out.at[side],
            dst_ref=edge_in.at[1 - side],
            send_sem=e_send.at[side],
            recv_sem=e_recv.at[1 - side],
            device_id=(me, up if side == 0 else down),
            device_id_type=MESH,
        )

    @pl.when(has_up)
    def _():
        edge_copy(0).start()

    @pl.when(has_down)
    def _():
        edge_copy(1).start()

    @pl.when(has_up)
    def _():
        edge_copy(1).wait_recv()

    @pl.when(has_down)
    def _():
        edge_copy(0).wait_recv()

    def summed(kind):
        here = looks[kind * look_rows : (kind + 1) * look_rows, :]
        above = edge_in[0, 8 * kind : 8 * kind + 8, :]
        below = edge_in[1, 8 * kind : 8 * kind + 8, :]
        parts = [here[0:8] + above, here[look_rows - 8 :] + below]
        if look_rows > 16:
            parts.insert(1, here[8 : look_rows - 8])
        return jnp.concatenate(parts, axis=0)

    reference_power = summed(3 * dates)
    parts = [[], []]
    for d in range(dates):
        scale = 1.0 / jnp.sqrt(reference_power * summed(3 * d + 2) + EPS)
        for c in range(2):
            parts[c].append(summed(3 * d + c) * scale)
    gamma = jnp.concatenate(parts[0] + parts[1], axis=0)
    gamma = gamma.astype(jnp.bfloat16).astype(jnp.float32)
    used = 2 * dates * look_rows
    if used < LANE:
        gamma = jnp.concatenate([gamma, jnp.zeros((LANE - used, gamma.shape[1]), jnp.float32)], axis=0)
    turned = gamma.T
    for j in range(n):
        strip_out[j] = turned[j * strip : (j + 1) * strip, :]

    def strip_copy(to, slot):
        return pltpu.make_async_remote_copy(
            src_ref=strip_out.at[to],
            dst_ref=strip_in.at[slot],
            send_sem=s_send.at[to],
            recv_sem=s_recv.at[slot],
            device_id=(to, az),
            device_id_type=MESH,
        )

    def send_strip(s, _):
        strip_copy((me + s) % n, me).start()
        return 0

    lax.fori_loop(1, n, send_strip, 0)
    strip_in[me] = strip_out[me]

    @pl.when(has_up)
    def _():
        rim_copy(0).wait_send()
        edge_copy(0).wait_send()

    @pl.when(has_down)
    def _():
        rim_copy(1).wait_send()
        edge_copy(1).wait_send()

    for part, last, to in ((0, chips - 1, onward), (1, 1, back)):

        @pl.when((core == 0) & (pos != last))
        def _():
            for i in range(per_part):
                chunk_copy(i, part, center, to, c_ring).wait_send()

        if pair == 2:

            @pl.when(core == 0)
            def _():
                for i in range(per_part):
                    chunk_copy(i, part, center, sibling, c_core).wait_send()

    def hear_strip(s, _):
        other = (me + s) % n
        strip_copy(other, other).wait_recv()
        strip_copy(other, other).wait_send()
        return 0

    lax.fori_loop(1, n, hear_strip, 0)

    half = dates * look_rows
    coh_ref[...] = strip_in[...]

    def magnitude(j, total):
        v = strip_in[j]
        sq = v * v
        return total + jnp.sqrt(sq[:, 0:half] + sq[:, half : 2 * half])

    total = lax.fori_loop(0, n, magnitude, jnp.zeros((strip, half), jnp.float32))
    mean = total[:, 0:look_rows]
    for d in range(1, dates):
        mean = mean + total[:, d * look_rows : (d + 1) * look_rows]
    mean_ref[...] = mean * (1.0 / (n * dates))


def body(n, n_az, slc, az_shift, rg_shift, az_frac, rg_frac):
    dates, _, rows, cols = slc.shape
    kinds = 3 * dates + 1
    look_rows, look_cols = rows // LOOK_AZ, cols // LOOK_RG
    lanes = -(-look_cols // LANE) * LANE
    strip = look_cols // n
    wide = -(-2 * dates * look_rows // LANE) * LANE
    per_part = rows // CHUNK
    bf, f32 = jnp.bfloat16, jnp.float32
    smem = pl.BlockSpec(memory_space=pltpu.SMEM)
    vmem = pl.BlockSpec(memory_space=pltpu.VMEM)
    anym = pl.BlockSpec(memory_space=pl.ANY)
    dma = pltpu.SemaphoreType.DMA
    strips, mean = pl.pallas_call(
        functools.partial(kernel, n, n_az, dates, rows, cols),
        out_shape=(
            jax.ShapeDtypeStruct((n, strip, wide), f32),
            jax.ShapeDtypeStruct((strip, look_rows), f32),
        ),
        in_specs=[smem] * 5 + [anym, anym, vmem],
        out_specs=(vmem, vmem),
        scratch_shapes=[
            pltpu.VMEM((dates, 2 * rows, cols + 2 * LANE), bf),
            pltpu.VMEM((2, dates, 2 * RIM, cols), bf),
            pltpu.VMEM((2, dates, 2 * RIM, cols + 2 * LANE), bf),
            pltpu.VMEM((2, rows, cols), bf),
            pltpu.VMEM((cols, lanes), bf),
            pltpu.VMEM((dates, 2, 2 * BLOCK, BLOCK), bf),
            pltpu.VMEM((dates, 4 * rows, 2 * rows + 4 * RIM), bf),
            pltpu.VMEM((dates, 2 * rows + 4 * RIM, cols), bf),
            pltpu.VMEM((dates, 2 * rows, cols), bf),
            pltpu.VMEM((kinds * rows, cols), bf),
            pltpu.VMEM((kinds * (look_rows + 16), lanes), f32),
            pltpu.VMEM((2, 8 * kinds, lanes), f32),
            pltpu.VMEM((2, 8 * kinds, lanes), f32),
            pltpu.VMEM((n, strip, wide), f32),
            pltpu.VMEM((n, strip, wide), f32),
            dma((dates, 2)),
            dma,
            dma,
            dma((2,)),
            dma((2,)),
            dma((2, per_part)),
            dma((2, per_part)),
            dma((2, per_part)),
            dma((2,)),
            dma((2,)),
            dma((n,)),
            dma((n,)),
        ],
        compiler_params=pltpu.CompilerParams(
            collective_id=0, has_side_effects=True, vmem_limit_bytes=48 * 1024 * 1024
        ),
    )(
        az_shift, rg_shift, az_frac, rg_frac, jnp.asarray(kernel_bank()), slc,
        column_boxes(cols, lanes), row_boxes(kinds, rows),
    )
    strips = strips[:, :, : 2 * dates * look_rows].reshape(n, strip, 2, dates, look_rows)
    coherence = jnp.transpose(strips, (1, 4, 2, 0, 3)).reshape(strip, look_rows, 2, n * dates)
    return coherence.astype(jnp.bfloat16), mean


def solution(mesh):
    placed = (P("date", None, "az", None), P("date"), P("date"), P("date"), P("date"))
    return jax.shard_map(
        functools.partial(body, mesh.shape["date"], mesh.shape["az"]),
        mesh=mesh,
        in_specs=placed,
        out_specs=(P("date", "az", None, None), P("date", "az")),
        check_vma=False,
    )
```

time: 196 us -> 52.4 us (0.27)
  local copies, waits for them, and re-layouts: 69.5 us -> 8.56 us
  between operations: 54.3 us -> 0.68 us
  other arithmetic: 47.1 us -> 0 us
  Pallas kernels: 0 us -> 42.9 us
  starting transfers between devices: 12.7 us -> 0 us
  blocking collectives: 8.73 us -> 0 us
    another operation x12 -> x0, local copies, waits for them, and re-layouts: 57.9 us -> none  [form_looks(): pieces.append(looks_of(jnp.stack([real_part, imag_part, power_sec])))]
    pallas_call x0 -> x1, Pallas kernels: none -> 42.9 us  [body(): pl.pallas_call(functools.partial(kernel, n, n_az, dates, rows, cols), out...]
    add x8 -> x0, other arithmetic: 38.7 us -> none  [the longest x2 20.2 us: form_looks(): ranged + rg_weights[date_pos, tap_place] * lax.dynamic_slice_in_dim(widen...]
    ppermute x4 -> x0, starting transfers between devices: 12.7 us -> none  [the longest x2 10.1 us: extended(): lax.ppermute(tail, axis, [(i, (i + 1) % count) for i in range(ends)])]
    all_to_all x1 -> x0, blocking collectives: 8.73 us -> none  [body(): lax.all_to_all(outgoing, 'date', split_axis=0, concat_axis=3, tiled=True)]
    unnamed x25 -> x18, local copies, waits for them, and re-layouts: 2.49 us -> 8.42 us
    add x1 -> x0, local copies, waits for them, and re-layouts: 4.89 us -> none  [form_looks(): power_ref = looks_of(center_re * center_re + center_im * center_im)[None]]
    reduce_sum x5 -> x0, other arithmetic: 4.61 us -> none  [the longest x3 4.42 us: looks_of(): return jnp.mean(boxed, axis=(-3, -1))]
  transfers between devices with their start and end apart: 5 -> 0, of which waited for: 1 -> 0; matrix products, arithmetic and copies ran while one was open for 21% -> 0% of each run, Pallas kernels for 0% -> 0%
where the time goes in v1:
time: 52.4 us; the launch traced here: 52.1 us
  Pallas kernels  42.9 us (82%)
  local copies, waits for them, and re-layouts  8.56 us (16%)
  between operations  0.68 us (1%)
    pallas_call x1, Pallas kernels, body(): pl.pallas_call(functools.partial(kernel, n, n_az, dates, rows, cols), out...  42.9 us
    unnamed x18, local copies, waits for them, and re-layouts  8.42 us

profile of v1, /device:TPU:0, one launch (start us, length us, event | category | flops | bytes accessed | tf_op | source)
XLA Modules:
  0.0 52.1 jit_solution(13021535580687698011)
XLA Ops:
  0.6 0.0 copy-start
  0.6 1.4 %copy-done = bf16[2,2,64,3072]{3,2,1,0:T(8,128)(2,1)S(1)} copy-done((bf16[2,2,64,3072]{3,2,1,0:T(8,128)(2,1)S(1)}, bf16[2,2,64,3072]{3,2,1,0:T(8,128)(2,1)}, u32[]{:S(2)}) %copy-start) | copy-done | bytes 1572888
  2.0 0.0 copy-start.1
  2.0 1.4 %copy-done.1 = bf16[3072,256]{1,0:T(8,128)(2,1)S(1)} copy-done((bf16[3072,256]{1,0:T(8,128)(2,1)S(1)}, bf16[3072,256]{1,0:T(8,128)(2,1)}, u32[]{:S(2)}) %copy-start.1) | copy-done | bytes 1572888
  3.4 0.0 copy-start.2
  3.5 0.9 %copy-done.2 = bf16[224,448]{1,0:T(8,128)(2,1)S(1)} copy-done((bf16[224,448]{1,0:T(8,128)(2,1)S(1)}, bf16[224,448]{1,0:T(8,128)(2,1)}, u32[]{:S(2)}) %copy-start.2) | copy-done | bytes 200728
  4.4 0.0 copy-start.3
  4.4 0.7 %copy-done.3 = f32[16,8]{1,0:T(8,128)S(1)} copy-done((f32[16,8]{1,0:T(8,128)S(1)}, f32[16,8]{1,0:T(8,128)}, u32[]{:S(2)}) %copy-start.3) | copy-done | bytes 536
  5.1 0.0 copy-start.4
  5.1 0.7 %copy-done.4 = s32[2]{0:T(128)S(1)} copy-done((s32[2]{0:T(128)S(1)}, s32[2]{0:T(128)}, u32[]{:S(2)}) %copy-start.4) | copy-done | bytes 32
  5.7 0.0 copy-start.5
  5.7 0.7 %copy-done.5 = s32[2]{0:T(128)S(1)} copy-done((s32[2]{0:T(128)S(1)}, s32[2]{0:T(128)}, u32[]{:S(2)}) %copy-start.5) | copy-done | bytes 32
  6.4 0.0 copy-start.6
  6.4 0.7 %copy-done.6 = s32[2]{0:T(128)S(1)} copy-done((s32[2]{0:T(128)S(1)}, s32[2]{0:T(128)}, u32[]{:S(2)}) %copy-start.6) | copy-done | bytes 32
  7.1 0.0 copy-start.7
  7.1 0.7 %copy-done.7 = s32[2]{0:T(128)S(1)} copy-done((s32[2]{0:T(128)S(1)}, s32[2]{0:T(128)}, u32[]{:S(2)}) %copy-start.7) | copy-done | bytes 32
  7.7 42.9 %shard_map.95 = (f32[8,24,128]{2,1,0:T(8,128)S(1)}, f32[24,16]{1,0:T(8,128)S(1)}) custom-call(s32[2]{0:T(128)S(1)} %copy-done.4, s32[2]{0:T(128)S(1)} %copy-done.5, s32[2]{0:T(128)S(1)} %copy-done.6, s32[2]{0:T(128)S(1)} %copy-done.7, f32[16,8]{1,0:T(8,128)S(1)} %copy-done.3, bf16[2,2,64,3072]{3,2,1,0:T(8,128)(2,1)S(1)} %copy-done, ...), custom_call_target="tpu_custom_call" | custom-call | tf_op jit(solution)/shard_map/pallas_call | solution.py:451
  50.6 0.7 %copy.17 = f32[24,16]{0,1:T(8,128)} copy(f32[24,16]{1,0:T(8,128)S(1)} %get-tuple-element.11) | data formatting | bytes 3072
  51.3 0.1 copy.14
  51.5 0.7 %copy.16 = bf16[24,16,2,16]{0,3,2,1:T(8,128)(2,1)} copy(bf16[24,16,2,16]{0,1,3,2:T(8,128)(2,1)S(1)} %bitcast.5) | data formatting | bytes 49152
  (2 shorter events, 0.0 us)
Async XLA Ops:
  0.6 1.4 %copy-start = (bf16[2,2,64,3072]{3,2,1,0:T(8,128)(2,1)S(1)}, bf16[2,2,64,3072]{3,2,1,0:T(8,128)(2,1)}, u32[]{:S(2)}) copy-start(bf16[2,2,64,3072]{3,2,1,0:T(8,128)(2,1)} %slc.1) | copy-start | bytes 4718596
  2.0 1.4 %copy-start.1 = (bf16[3072,256]{1,0:T(8,128)(2,1)S(1)}, bf16[3072,256]{1,0:T(8,128)(2,1)}, u32[]{:S(2)}) copy-start(bf16[3072,256]{1,0:T(8,128)(2,1)} %constant.7.clone.boxes_hbm) | copy-start | bytes 4718596
  3.4 0.9 %copy-start.2 = (bf16[224,448]{1,0:T(8,128)(2,1)S(1)}, bf16[224,448]{1,0:T(8,128)(2,1)}, u32[]{:S(2)}) copy-start(bf16[224,448]{1,0:T(8,128)(2,1)} %constant.8.clone.row_box) | copy-start | bytes 602116
  4.4 0.7 %copy-start.3 = (f32[16,8]{1,0:T(8,128)S(1)}, f32[16,8]{1,0:T(8,128)}, u32[]{:S(2)}) copy-start(f32[16,8]{1,0:T(8,128)} %constant.6.clone.bank) | copy-start | bytes 1540
  5.1 0.7 %copy-start.4 = (s32[2]{0:T(128)S(1)}, s32[2]{0:T(128)}, u32[]{:S(2)}) copy-start(s32[2]{0:T(128)} %az_shift.1) | copy-start | bytes 28
  5.7 0.7 %copy-start.5 = (s32[2]{0:T(128)S(1)}, s32[2]{0:T(128)}, u32[]{:S(2)}) copy-start(s32[2]{0:T(128)} %rg_shift.1) | copy-start | bytes 28
  6.4 0.7 %copy-start.6 = (s32[2]{0:T(128)S(1)}, s32[2]{0:T(128)}, u32[]{:S(2)}) copy-start(s32[2]{0:T(128)} %az_frac.1) | copy-start | bytes 28
  7.1 0.7 %copy-start.7 = (s32[2]{0:T(128)S(1)}, s32[2]{0:T(128)}, u32[]{:S(2)}) copy-start(s32[2]{0:T(128)} %rg_frac.1) | copy-start | bytes 28

commit v2 on v1

--- a/solution.py
+++ b/solution.py
@@ -22,6 +22,7 @@
 LANE = 128
 BLOCK = 2 * LANE
 CHUNK = 16
+PIECES = 4
 MESH = pl.DeviceIdType.MESH
 
 
@@ -80,16 +81,17 @@
     load_sem, box_sem, own_sem, rim_send, rim_recv, c_ring, c_core, c_recv, e_send, e_recv, s_send, s_recv,
 ):
     me, az = lax.axis_index("date"), lax.axis_index("az")
-    pair = 2 if n % 2 == 0 and n >= 4 else 1
-    chips = n // pair
-    chip, core = me // pair, me % pair
+    chips = n // 2
+    chip, core = me // 2, me % 2
+    n_pieces = c_recv.shape[2]
+    piece = 2 * cols // n_pieces
 
     def snake(p):
         return (p // 2) * 2 + (p + p // 2) % 2
 
     pos = snake(chip)
-    onward = snake((pos + 1) % chips) * pair + core
-    back = snake((pos + chips - 1) % chips) * pair + core
+    onward = snake((pos + 1) % chips) * 2 + core
+    back = snake((pos + chips - 1) % chips) * 2 + core
     up, down = jnp.maximum(az - 1, 0), jnp.minimum(az + 1, n_az - 1)
     has_up, has_down = az > 0, az < n_az - 1
 
@@ -166,36 +168,41 @@
             device_id_type=MESH,
         )
 
-    per_part = rows // CHUNK
-
-    def place(i, part):
-        return i % 2, pl.ds(pl.multiple_of((i // 2) * CHUNK + part * (rows // 2), CHUNK), CHUNK)
-
-    def chunk_copy(i, part, source, to, sems):
-        c, r = place(i, part)
+    def place(i, way, stream):
+        r = pl.multiple_of(way * (rows // 2) + stream * (rows // 4), CHUNK)
+        c = pl.multiple_of((i // 2) * piece, LANE)
+        return i % 2, pl.ds(r, rows // 4), pl.ds(c, piece)
+
+    def chunk_copy(i, way, stream, source, to, send_sem):
+        where = place(i, way, stream)
         return pltpu.make_async_remote_copy(
-            src_ref=source.at[c, r, :],
-            dst_ref=center.at[c, r, :],
-            send_sem=sems.at[part, i],
-            recv_sem=c_recv.at[part, i],
+            src_ref=source.at[where],
+            dst_ref=center.at[where],
+            send_sem=send_sem,
+            recv_sem=c_recv.at[way, stream, i],
             device_id=(to, az),
             device_id_type=MESH,
         )
 
+    def ring_copy(i, way, stream, source):
+        return chunk_copy(i, way, stream, source, onward if way == 0 else back, c_ring.at[way, i])
+
+    def core_copy(i, way, stream, source):
+        return chunk_copy(i, way, stream, source, sibling, c_core.at[way, stream, i])
+
     is_source = jnp.logical_and(pos == 0, core == 0)
-    relay = jnp.logical_and(pos > 0, core == 0)
-    sibling = chip * pair + 1
+    sibling = chip * 2 + (1 - core)
     own_center = pltpu.make_async_copy(slc.at[0], center, own_sem)
 
     @pl.when(is_source)
     def _():
-        for i in range(per_part):
-            for part, to in ((0, onward), (1, back)):
-                chunk_copy(i, part, slc.at[0], to, c_ring).start()
-        for i in range(per_part):
-            for part in range(2):
-                if pair == 2:
-                    chunk_copy(i, part, slc.at[0], sibling, c_core).start()
+        for i in range(n_pieces):
+            for way in range(2):
+                core_copy(i, way, 1, slc.at[0]).start()
+                ring_copy(i, way, 0, slc.at[0]).start()
+        for i in range(n_pieces):
+            for way in range(2):
+                core_copy(i, way, 0, slc.at[0]).start()
         own_center.start()
 
     @pl.when(has_up)
@@ -207,20 +214,22 @@
         rim_copy(1).start()
 
     def relay_step(t):
-        for part, i, last, to in ((0, t - pos, chips - 1, onward), (1, t - (chips - pos), 1, back)):
-
-            @pl.when(relay & (i >= 0) & (i < per_part))
+        for way, hops, last in ((0, pos, chips - 1), (1, (chips - pos) % chips, 1)):
+            i = t - hops - core
+
+            @pl.when(jnp.logical_not(is_source) & (i >= 0) & (i < n_pieces))
             def _():
-                chunk_copy(i, part, center, to, c_ring).wait_recv()
+                ring_copy(i, way, core, center).wait_recv()
 
                 @pl.when(pos != last)
                 def _():
-                    chunk_copy(i, part, center, to, c_ring).start()
-
-                if pair == 2:
-                    chunk_copy(i, part, center, sibling, c_core).start()
-
-    steps = [functools.partial(relay_step, t) for t in range(1, chips + per_part - 1)]
+                    ring_copy(i, way, core, center).start()
+
+                @pl.when(pos > 0)
+                def _():
+                    core_copy(i, way, core, center).start()
+
+    steps = [functools.partial(relay_step, t) for t in range(1, chips + n_pieces)]
 
     for d in range(dates):
         weights = [bank[rg_frac[d], j] for j in range(TAPS)]
@@ -260,28 +269,26 @@
             ranged[d, 0 : 2 * rows, here] = (dot(x, toep[d, 0]) + dot(x, toep[d, 1])).astype(jnp.bfloat16)
         return 0
 
-    done = 0
-    for t, step in enumerate(steps):
-        step()
-        until = min(n_blocks, -(-n_blocks * (t + 1) // min(len(steps), 4)))
-        if until > done:
-            lax.fori_loop(done, until, range_block, 0)
-            done = until
-
-    @pl.when(has_up)
-    def _():
-        rim_copy(1).wait_recv()
-
-    @pl.when(has_down)
-    def _():
-        rim_copy(0).wait_recv()
+    def range_rims(_):
+        @pl.when(has_up)
+        def _():
+            rim_copy(1).wait_recv()
+
+        @pl.when(has_down)
+        def _():
+            rim_copy(0).wait_recv()
+
+        for d in range(dates):
+            x = jnp.concatenate(
+                [rim_in[side, d, :, k * BLOCK : (k + 2) * BLOCK] for k in range(n_blocks) for side in range(2)], axis=0
+            )
+            y = (dot(x, toep[d, 0]) + dot(x, toep[d, 1])).astype(jnp.bfloat16)
+            for k in range(n_blocks):
+                ranged[d, 2 * rows :, k * BLOCK : (k + 1) * BLOCK] = y[4 * RIM * k : 4 * RIM * (k + 1)]
 
     def az_block(k, _):
-        window = pl.ds(pl.multiple_of(k * BLOCK, LANE), 2 * BLOCK)
         here = pl.ds(pl.multiple_of(k * BLOCK, LANE), BLOCK)
         for d in range(dates):
-            x = jnp.concatenate([rim_in[0, d, :, window], rim_in[1, d, :, window]], axis=0)
-            ranged[d, 2 * rows :, here] = (dot(x, toep[d, 0]) + dot(x, toep[d, 1])).astype(jnp.bfloat16)
             both = dot(azm[d], ranged[d, :, here])
             s = both[0 : 2 * rows] + both[2 * rows :]
             sec[d, :, here] = s.astype(jnp.bfloat16)
@@ -289,17 +296,25 @@
             prod[(3 * d + 2) * rows : (3 * d + 3) * rows, here] = power.astype(jnp.bfloat16)
         return 0
 
-    lax.fori_loop(0, n_blocks, az_block, 0)
+    third = n_blocks // 3
+    work = [functools.partial(lax.fori_loop, k * third, (k + 1) * third, range_block) for k in range(3)]
+    work += [range_rims]
+    work += [functools.partial(lax.fori_loop, k * third, (k + 1) * third, az_block) for k in range(3)]
+    for k in range(max(len(steps), len(work))):
+        if k < len(work):
+            work[k](0)
+        if k < len(steps):
+            steps[k]()
 
     @pl.when(is_source)
     def _():
         own_center.wait()
 
-    @pl.when(core != 0)
-    def _():
-        for i in range(per_part):
-            for part in range(2):
-                chunk_copy(i, part, center, onward, c_ring).wait_recv()
+    @pl.when(jnp.logical_not(is_source))
+    def _():
+        for i in range(n_pieces):
+            for way in range(2):
+                core_copy(i, way, 1 - core, center).wait_recv()
 
     def cross_block(k, _):
         here = pl.ds(pl.multiple_of(k * BLOCK, LANE), BLOCK)
@@ -363,13 +378,9 @@
         for c in range(2):
             parts[c].append(summed(3 * d + c) * scale)
     gamma = jnp.concatenate(parts[0] + parts[1], axis=0)
-    gamma = gamma.astype(jnp.bfloat16).astype(jnp.float32)
-    used = 2 * dates * look_rows
-    if used < LANE:
-        gamma = jnp.concatenate([gamma, jnp.zeros((LANE - used, gamma.shape[1]), jnp.float32)], axis=0)
-    turned = gamma.T
+    gamma = gamma.astype(jnp.bfloat16)
     for j in range(n):
-        strip_out[j] = turned[j * strip : (j + 1) * strip, :]
+        strip_out[j] = gamma[:, j * strip : (j + 1) * strip]
 
     def strip_copy(to, slot):
         return pltpu.make_async_remote_copy(
@@ -398,19 +409,24 @@
         rim_copy(1).wait_send()
         edge_copy(1).wait_send()
 
-    for part, last, to in ((0, chips - 1, onward), (1, 1, back)):
-
-        @pl.when((core == 0) & (pos != last))
+    for way, last in ((0, chips - 1), (1, 1)):
+
+        @pl.when(pos != last)
         def _():
-            for i in range(per_part):
-                chunk_copy(i, part, center, to, c_ring).wait_send()
-
-        if pair == 2:
-
-            @pl.when(core == 0)
-            def _():
-                for i in range(per_part):
-                    chunk_copy(i, part, center, sibling, c_core).wait_send()
+            for i in range(n_pieces):
+                ring_copy(i, way, core, center).wait_send()
+
+        @pl.when(pos > 0)
+        def _():
+            for i in range(n_pieces):
+                core_copy(i, way, core, center).wait_send()
+
+    @pl.when(is_source)
+    def _():
+        for i in range(n_pieces):
+            for way in range(2):
+                for stream in range(2):
+                    core_copy(i, way, stream, center).wait_send()
 
     def hear_strip(s, _):
         other = (me + s) % n
@@ -424,14 +440,14 @@
     coh_ref[...] = strip_in[...]
 
     def magnitude(j, total):
-        v = strip_in[j]
+        v = strip_in[j].astype(jnp.float32)
         sq = v * v
-        return total + jnp.sqrt(sq[:, 0:half] + sq[:, half : 2 * half])
-
-    total = lax.fori_loop(0, n, magnitude, jnp.zeros((strip, half), jnp.float32))
-    mean = total[:, 0:look_rows]
+        return total + jnp.sqrt(sq[0:half] + sq[half : 2 * half])
+
+    total = lax.fori_loop(0, n, magnitude, jnp.zeros((half, strip), jnp.float32))
+    mean = total[0:look_rows]
     for d in range(1, dates):
-        mean = mean + total[:, d * look_rows : (d + 1) * look_rows]
+        mean = mean + total[d * look_rows : (d + 1) * look_rows]
     mean_ref[...] = mean * (1.0 / (n * dates))
 
 
@@ -441,8 +457,7 @@
     look_rows, look_cols = rows // LOOK_AZ, cols // LOOK_RG
     lanes = -(-look_cols // LANE) * LANE
     strip = look_cols // n
-    wide = -(-2 * dates * look_rows // LANE) * LANE
-    per_part = rows // CHUNK
+    tall = 2 * dates * look_rows
     bf, f32 = jnp.bfloat16, jnp.float32
     smem = pl.BlockSpec(memory_space=pltpu.SMEM)
     vmem = pl.BlockSpec(memory_space=pltpu.VMEM)
@@ -451,8 +466,8 @@
     strips, mean = pl.pallas_call(
         functools.partial(kernel, n, n_az, dates, rows, cols),
         out_shape=(
-            jax.ShapeDtypeStruct((n, strip, wide), f32),
-            jax.ShapeDtypeStruct((strip, look_rows), f32),
+            jax.ShapeDtypeStruct((n, tall, strip), bf),
+            jax.ShapeDtypeStruct((look_rows, strip), f32),
         ),
         in_specs=[smem] * 5 + [anym, anym, vmem],
         out_specs=(vmem, vmem),
@@ -470,31 +485,31 @@
             pltpu.VMEM((kinds * (look_rows + 16), lanes), f32),
             pltpu.VMEM((2, 8 * kinds, lanes), f32),
             pltpu.VMEM((2, 8 * kinds, lanes), f32),
-            pltpu.VMEM((n, strip, wide), f32),
-            pltpu.VMEM((n, strip, wide), f32),
+            pltpu.VMEM((n, tall, strip), bf),
+            pltpu.VMEM((n, tall, strip), bf),
             dma((dates, 2)),
             dma,
             dma,
             dma((2,)),
             dma((2,)),
-            dma((2, per_part)),
-            dma((2, per_part)),
-            dma((2, per_part)),
+            dma((2, PIECES)),
+            dma((2, 2, PIECES)),
+            dma((2, 2, PIECES)),
             dma((2,)),
             dma((2,)),
             dma((n,)),
             dma((n,)),
         ],
         compiler_params=pltpu.CompilerParams(
-            collective_id=0, has_side_effects=True, vmem_limit_bytes=48 * 1024 * 1024
+            collective_id=0, has_side_effects=True, vmem_limit_bytes=60 * 1024 * 1024
         ),
     )(
         az_shift, rg_shift, az_frac, rg_frac, jnp.asarray(kernel_bank()), slc,
         column_boxes(cols, lanes), row_boxes(kinds, rows),
     )
-    strips = strips[:, :, : 2 * dates * look_rows].reshape(n, strip, 2, dates, look_rows)
-    coherence = jnp.transpose(strips, (1, 4, 2, 0, 3)).reshape(strip, look_rows, 2, n * dates)
-    return coherence.astype(jnp.bfloat16), mean
+    strips = strips.reshape(n, 2, dates, look_rows, strip)
+    coherence = jnp.transpose(strips, (4, 3, 1, 0, 2)).reshape(strip, look_rows, 2, n * dates)
+    return coherence, mean.T
 
 
 def solution(mesh):

time: 52.4 us -> 37.6 us (0.72)
  Pallas kernels: 42.9 us -> 33.8 us
  local copies, waits for them, and re-layouts: 8.56 us -> 2.96 us
    pallas_call x1, Pallas kernels: 42.9 us -> 33.8 us  [body(): pl.pallas_call(functools.partial(kernel, n, n_az, dates, rows, cols), out...]
    unnamed x18 -> x1, local copies, waits for them, and re-layouts: 8.42 us -> 1.29 us
    transpose x0 -> x1, local copies, waits for them, and re-layouts: none -> 1.66 us  [body(): jnp.transpose(strips, (4, 3, 1, 0, 2))]
where the time goes in v2:
time: 37.6 us; the launch traced here: 37.4 us
  Pallas kernels  33.8 us (90%)
  local copies, waits for them, and re-layouts  2.96 us (8%)
  between operations  0.64 us (2%)
    pallas_call x1, Pallas kernels, body(): pl.pallas_call(functools.partial(kernel, n, n_az, dates, rows, cols), out...  33.8 us
    transpose x1, local copies, waits for them, and re-layouts, body(): jnp.transpose(strips, (4, 3, 1, 0, 2))  1.66 us
    unnamed x1, local copies, waits for them, and re-layouts  1.29 us

profile of v2, /device:TPU:0, one launch (start us, length us, event | category | flops | bytes accessed | tf_op | source)
XLA Modules:
  0.0 37.4 jit_solution(17457177102306085326)
XLA Ops:
  0.6 33.8 %shard_map.95 = (bf16[8,64,24]{2,1,0:T(8,128)(2,1)}, f32[16,24]{1,0:T(8,128)}) custom-call(s32[2]{0:T(128)} %az_shift.1, s32[2]{0:T(128)} %rg_shift.1, s32[2]{0:T(128)} %az_frac.1, s32[2]{0:T(128)} %rg_frac.1, f32[16,8]{1,0:T(8,128)} %constant.6.clone.bank, bf16[2,2,64,3072]{3,2,1,0:T(8,128)(2,1)} %slc.1, bf16[3072,256]{1,0:T(8,128)(2,1)} %constant.7.clone.boxes_hbm, ...), custom_call_target="tpu_custom_call" | custom-call | tf_op jit(solution)/shard_map/pallas_call | solution.py:466
  34.5 1.7 %copy.10 = bf16[24,16,2,8,2]{0,4,3,2,1:T(2,128)(2,1)} copy(bf16[24,16,2,8,2]{0,1,4,2,3:T(8,128)(2,1)} %bitcast.6) | data formatting | bytes 49152 | tf_op jit(solution)/shard_map/transpose | solution.py:511
  36.1 1.3 %copy.12 = f32[24,16]{0,1:T(8,128)} copy(f32[24,16]{0,1:T(8,128)} %bitcast.7) | data formatting | bytes 3072

commit v3 on v2

--- a/solution.py
+++ b/solution.py
@@ -90,8 +90,8 @@
         return (p // 2) * 2 + (p + p // 2) % 2
 
     pos = snake(chip)
-    onward = snake((pos + 1) % chips) * 2 + core
-    back = snake((pos + chips - 1) % chips) * 2 + core
+    onward = snake((pos + 1) % chips) * 2
+    back = snake((pos + chips - 1) % chips) * 2
     up, down = jnp.maximum(az - 1, 0), jnp.minimum(az + 1, n_az - 1)
     has_up, has_down = az > 0, az < n_az - 1
 
@@ -142,18 +142,6 @@
     def _():
         rim_in[1, :, :, LANE : LANE + cols] = jnp.zeros((dates, 2 * RIM, cols), jnp.bfloat16)
         edge_in[1] = jnp.zeros(edge_in.shape[1:], jnp.float32)
-
-    for load in loads:
-        load.wait()
-
-    for d in range(dates):
-        for side, lo in ((0, 0), (1, rows - 16)):
-            cut = slice(0, RIM) if side == 0 else slice(16 - RIM, 16)
-            both = [
-                own[d, c * rows + lo : c * rows + lo + 16, LANE : LANE + cols].astype(jnp.float32)[cut]
-                for c in range(2)
-            ]
-            rim_out[side, d] = jnp.concatenate(both, axis=0).astype(jnp.bfloat16)
 
     n_here = has_up.astype(jnp.int32) + has_down.astype(jnp.int32)
     pl.semaphore_wait(barrier, n - 1 + n_here)
@@ -185,7 +173,7 @@
         )
 
     def ring_copy(i, way, stream, source):
-        return chunk_copy(i, way, stream, source, onward if way == 0 else back, c_ring.at[way, i])
+        return chunk_copy(i, way, stream, source, (onward if way == 0 else back) + stream, c_ring.at[way, stream, i])
 
     def core_copy(i, way, stream, source):
         return chunk_copy(i, way, stream, source, sibling, c_core.at[way, stream, i])
@@ -198,13 +186,26 @@
     def _():
         for i in range(n_pieces):
             for way in range(2):
-                core_copy(i, way, 1, slc.at[0]).start()
-                ring_copy(i, way, 0, slc.at[0]).start()
+                for stream in range(2):
+                    ring_copy(i, way, stream, slc.at[0]).start()
         for i in range(n_pieces):
             for way in range(2):
-                core_copy(i, way, 0, slc.at[0]).start()
+                for stream in range(2):
+                    core_copy(i, way, stream, slc.at[0]).start()
         own_center.start()
 
+    for load in loads:
+        load.wait()
+
+    for d in range(dates):
+        for side, lo in ((0, 0), (1, rows - 16)):
+            cut = slice(0, RIM) if side == 0 else slice(16 - RIM, 16)
+            both = [
+                own[d, c * rows + lo : c * rows + lo + 16, LANE : LANE + cols].astype(jnp.float32)[cut]
+                for c in range(2)
+            ]
+            rim_out[side, d] = jnp.concatenate(both, axis=0).astype(jnp.bfloat16)
+
     @pl.when(has_up)
     def _():
         rim_copy(0).start()
@@ -214,10 +215,10 @@
         rim_copy(1).start()
 
     def relay_step(t):
-        for way, hops, last in ((0, pos, chips - 1), (1, (chips - pos) % chips, 1)):
-            i = t - hops - core
-
-            @pl.when(jnp.logical_not(is_source) & (i >= 0) & (i < n_pieces))
+        for way, hops, last in ((0, pos, chips - 1), (1, chips - pos, 1)):
+            i = t - hops
+
+            @pl.when((pos > 0) & (i >= 0) & (i < n_pieces))
             def _():
                 ring_copy(i, way, core, center).wait_recv()
 
@@ -225,11 +226,9 @@
                 def _():
                     ring_copy(i, way, core, center).start()
 
-                @pl.when(pos > 0)
-                def _():
-                    core_copy(i, way, core, center).start()
-
-    steps = [functools.partial(relay_step, t) for t in range(1, chips + n_pieces)]
+                core_copy(i, way, core, center).start()
+
+    steps = [functools.partial(relay_step, t) for t in range(1, chips + n_pieces - 1)]
 
     for d in range(dates):
         weights = [bank[rg_frac[d], j] for j in range(TAPS)]
@@ -316,6 +315,12 @@
             for way in range(2):
                 core_copy(i, way, 1 - core, center).wait_recv()
 
+    @pl.when((pos == 0) & (core != 0))
+    def _():
+        for i in range(n_pieces):
+            for way in range(2):
+                core_copy(i, way, core, center).wait_recv()
+
     def cross_block(k, _):
         here = pl.ds(pl.multiple_of(k * BLOCK, LANE), BLOCK)
         e0, e1 = center[0, :, here].astype(jnp.float32), center[1, :, here].astype(jnp.float32)
@@ -411,7 +416,7 @@
 
     for way, last in ((0, chips - 1), (1, 1)):
 
-        @pl.when(pos != last)
+        @pl.when((pos > 0) & (pos != last))
         def _():
             for i in range(n_pieces):
                 ring_copy(i, way, core, center).wait_send()
@@ -426,6 +431,7 @@
         for i in range(n_pieces):
             for way in range(2):
                 for stream in range(2):
+                    ring_copy(i, way, stream, center).wait_send()
                     core_copy(i, way, stream, center).wait_send()
 
     def hear_strip(s, _):
@@ -492,7 +498,7 @@
             dma,
             dma((2,)),
             dma((2,)),
-            dma((2, PIECES)),
+            dma((2, 2, PIECES)),
             dma((2, 2, PIECES)),
             dma((2, 2, PIECES)),
             dma((2,)),

time: 37.6 us -> 37.8 us (level)
  no operation moved by 1% of the time
where the time goes in v3:
time: 37.8 us; the launch traced here: 37.6 us
  Pallas kernels  34 us (90%)
  local copies, waits for them, and re-layouts  2.96 us (8%)
  between operations  0.64 us (2%)
    pallas_call x1, Pallas kernels, body(): pl.pallas_call(functools.partial(kernel, n, n_az, dates, rows, cols), out...  34 us
    transpose x1, local copies, waits for them, and re-layouts, body(): jnp.transpose(strips, (4, 3, 1, 0, 2))  1.66 us
    unnamed x1, local copies, waits for them, and re-layouts  1.29 us

profile of v3, /device:TPU:0, one launch (start us, length us, event | category | flops | bytes accessed | tf_op | source)
XLA Modules:
  0.0 37.6 jit_solution(7508782949832475017)
XLA Ops:
  0.6 34.0 %shard_map.95 = (bf16[8,64,24]{2,1,0:T(8,128)(2,1)}, f32[16,24]{1,0:T(8,128)}) custom-call(s32[2]{0:T(128)} %az_shift.1, s32[2]{0:T(128)} %rg_shift.1, s32[2]{0:T(128)} %az_frac.1, s32[2]{0:T(128)} %rg_frac.1, f32[16,8]{1,0:T(8,128)} %constant.6.clone.bank, bf16[2,2,64,3072]{3,2,1,0:T(8,128)(2,1)} %slc.1, bf16[3072,256]{1,0:T(8,128)(2,1)} %constant.7.clone.boxes_hbm, ...), custom_call_target="tpu_custom_call" | custom-call | tf_op jit(solution)/shard_map/pallas_call | solution.py:472
  34.6 1.7 %copy.10 = bf16[24,16,2,8,2]{0,4,3,2,1:T(2,128)(2,1)} copy(bf16[24,16,2,8,2]{0,1,4,2,3:T(8,128)(2,1)} %bitcast.6) | data formatting | bytes 49152 | tf_op jit(solution)/shard_map/transpose | solution.py:517
  36.3 1.3 %copy.12 = f32[24,16]{0,1:T(8,128)} copy(f32[24,16]{0,1:T(8,128)} %bitcast.7) | data formatting | bytes 3072
